TPU v7x, 768 devices: a whole 4x8x12 slice. The times are simulated.
768 devices in a mesh: grid: 96 (over z_hi, x, y), depth: 8 (over z_lo, core).
Axes of the slice: x: 4, y: 8, z: 12 (z_hi: 3, z_lo: 4; z = z_hi * 4 + z_lo), core: 2. Of those that a mesh axis runs over, the one named last changes fastest.
Arguments:
- density: float32 [384, 8, 32, 32], P('grid', 'depth'), may hold values from -1 to 1
- columns: int32 [384, 8, 1], P('grid', 'depth'), may hold values from 0 to 47, as said below
- fill_columns: int32 [384, 8, 4], P('grid', 'depth'), may hold values from 0 to 47, as said below
Outputs:
- purified: float32 [384, 8, 32, 128], P('grid', 'depth')
Inputs may be any that keep to these rules, and one draw needn't show every extreme that they name: `columns`: the 1 entries of one block row and one column group are distinct. `fill_columns`: the 4 entries of one block row and one column group are distinct.
All inputs are finite; a program needn't handle non-finite values.
Results may differ from a plain program's by a relative error of at most 0.0003.
Values sent between devices are 32-bit elements; how exact they have to be, the bound alone decides.
No kernel may reach another device: no remote copies, remote signals or barrier semaphores. Data moves between devices by JAX's collectives and lax.ppermute only.
A program may use at most 32 MiB of HBM per device.

v0:
```python
import jax
import jax.numpy as jnp
from jax import lax
from jax.sharding import PartitionSpec as P


def multiply_tile(left, chosen_values, chosen_columns, own_fill):
    row_count, groups, block_size, width = left.shape
    slots = width // block_size
    shaped = left.reshape(row_count, groups, block_size, slots, block_size)
    left_blocks = shaped.transpose(0, 1, 3, 2, 4).reshape(
        row_count, groups * slots, block_size, block_size
    )
    right_slots = chosen_values.shape[3] // block_size
    right = chosen_values.reshape(row_count, groups * slots, block_size, right_slots, block_size)
    products = jnp.einsum("itab,itbsc->itsac", left_blocks, right, precision=lax.Precision.HIGHEST)
    match = (chosen_columns[:, :, :, None] == own_fill[:, None, None, :]).astype(jnp.float32)
    result = jnp.einsum("itsf,itsac->iafc", match, products, precision=lax.Precision.HIGHEST)
    return result.reshape(row_count, 1, block_size, own_fill.shape[1] * block_size)


def local(density, columns, fill_columns):
    row_count = density.shape[0]
    groups = lax.axis_size("depth")
    group_width = row_count * lax.axis_size("grid") // groups
    full_rows, row_columns, row_fill = (
        lax.all_gather(density, "depth", axis=1, tiled=True),
        lax.all_gather(columns, "depth", axis=1, tiled=True),
        lax.all_gather(fill_columns, "depth", axis=1, tiled=True),
    )
    offsets = jnp.arange(groups, dtype=jnp.int32)[None, :, None] * group_width
    first_need = (row_columns + offsets).reshape(row_count, -1)
    second_need = (row_fill + offsets).reshape(row_count, -1)
    own_fill = fill_columns[:, 0, :]
    gathered, gathered_columns = (
        lax.all_gather(density, "grid", axis=0, tiled=True),
        lax.all_gather(columns, "grid", axis=0, tiled=True),
    )
    gathered = gathered[:, 0]
    gathered_columns = gathered_columns[:, 0]
    first_values = gathered[first_need]
    first_columns = gathered_columns[first_need]
    second_values = gathered[second_need]
    second_columns = gathered_columns[second_need]
    squared = multiply_tile(full_rows, first_values, first_columns, own_fill)
    squared_rows = lax.all_gather(squared, "depth", axis=1, tiled=True)
    cubed = multiply_tile(squared_rows, second_values, second_columns, own_fill)
    return 3.0 * squared - 2.0 * cubed


def solution(mesh):
    in_specs = (P("grid", "depth", None, None), P("grid", "depth", None), P("grid", "depth", None))
    out_specs = P("grid", "depth", None, None)
    return jax.shard_map(local, mesh=mesh, in_specs=in_specs, out_specs=out_specs, check_vma=False)
```

profile of v0, /device:TPU:1, one launch (start us, length us, event | category | flops | bytes accessed | tf_op | source)
XLA Modules:
  0.0 454.7 jit_solution(10911646045640949148)
XLA Ops:
  6.5 0.0 copy-start.2
  6.5 0.0 all-gather.2.cloned.1.call-start
  6.5 0.7 all-gather.2.cloned.1.call-update
  7.3 18.9 %all_gather.19 = s32[4,8,1]{0,2,1:T(1,128)S(1)} all-gather(s32[4,1,1]{0,2,1:T(1,128)} %param.4), channel_id=1, replica_groups=mesh['grid'=96,'depth'=8] {'depth'}, dimensions={1}, use_global_device_ids=true | all-gather | bytes 144 | tf_op jit(solution)/shard_map/all_gather | solution.py:28
  26.2 0.1 compare_select_fusion
  26.2 0.1 copy.42
  26.3 0.1 reshape.111
  26.4 1.3 dynamic-slice
  28.4 0.8 bitcast_dynamic-update-slice_fusion
  29.1 317.9 %all-reduce = s32[384]{0:T(512)S(1)} all-reduce(s32[384]{0:T(512)S(1)} %bitcast_dynamic-update-slice_fusion), channel_id=1, replica_groups=mesh['grid'=96,'depth'=8] {'grid'}, use_global_device_ids=true, to_apply=%add | all-reduce | flops 384 | bytes 3072 | tf_op jit(solution)/shard_map/squeeze | solution.py:40
  347.0 0.0 copy-start.1
  347.1 0.7 gather_fusion.1
  347.8 0.1 eq.38
  347.8 0.0 copy-done.2
  347.8 46.5 %all_gather.22 = s32[4,8,4]{2,0,1:T(4,128)S(1)} all-gather(s32[4,1,4]{2,0,1:T(4,128)S(1)} %bitcast.52), channel_id=1, replica_groups=mesh['grid'=96,'depth'=8] {'depth'}, dimensions={1}, use_global_device_ids=true | all-gather | bytes 576 | tf_op jit(solution)/shard_map/all_gather | solution.py:29
  394.4 0.1 copy.46
  394.5 0.1 copy.47
  394.6 0.1 reshape.106
  394.7 0.1 reshape.129
  394.7 1.3 gather_fusion.3
  396.0 0.1 eq.43
  396.1 0.0 copy-done.1
  396.1 14.9 %all_gather.20 = f32[4,8,32,32]{3,2,1,0:T(8,128)S(1)} all-gather(f32[4,1,32,32]{3,2,1,0:T(8,128)S(1)} %copy-done.1), channel_id=1, replica_groups=mesh['grid'=96,'depth'=8] {'depth'}, dimensions={1}, use_global_device_ids=true | all-gather | bytes 147456 | tf_op jit(solution)/shard_map/all_gather | solution.py:27
  411.0 0.0 all-gather.2.cloned.1.call-done
  411.0 3.4 gather_fusion
  414.4 4.8 %gather_fusion.2 = f32[128,32,32]{2,1,0:T(8,128)} fusion(f32[384,32,32]{2,1,0:T(8,128)} %bitcast.51, s32[1024]{0:T(1024)S(1)} %pad_clamp_fusion), kind=kCustom, calls=%fused_computation.2 | custom fusion | bytes 1049088 | tf_op jit(solution)/shard_map/gather | solution.py:43
  419.2 1.0 convolution_bitcast_fusion.1
  420.3 0.2 copy.44
  420.5 0.4 convolution_bitcast_fusion.2
  420.9 0.2 reshape.105
  421.1 15.0 %all_gather.23 = f32[4,8,32,128]{3,2,0,1:T(8,128)S(1)} all-gather(f32[4,1,32,128]{3,2,0,1:T(8,128)S(1)} %reshape.105), channel_id=1, replica_groups=mesh['grid'=96,'depth'=8] {'depth'}, dimensions={1}, use_global_device_ids=true | all-gather | bytes 589824 | tf_op jit(solution)/shard_map/all_gather | solution.py:46
  436.0 0.5 fusion.9
  436.5 0.2 pad_maximum_fusion
  436.7 0.0 copy-start
  436.7 0.2 copy.48
  436.9 1.4 copy-done
  438.3 3.6 convolution_bitcast_fusion
  442.0 2.7 copy.50
  444.6 2.4 fusion
  447.0 0.2 mul.50
  447.2 0.6 subtract_bitcast_fusion
  (6 shorter events, 0.0 us)
Async XLA Ops:
  6.5 341.3 %copy-start.2 = (s32[4,1,4]{2,1,0:T(1,128)S(1)}, s32[4,1,4]{2,1,0:T(1,128)}, u32[]{:S(2)}) copy-start(s32[4,1,4]{2,1,0:T(1,128)} %param.5) | copy-start | bytes 196
  6.5 404.5 %all-gather.2.cloned.1.call-start = ((), (), s32[]{:S(2)}) async-start(), calls=%async_computation | async-start | bytes 6356992 | tf_op jit(solution)/shard_map/all_gather | solution.py:36
  347.0 49.1 %copy-start.1 = (f32[4,1,32,32]{3,2,1,0:T(8,128)S(1)}, f32[4,1,32,32]{3,2,1,0:T(8,128)}, u32[]{:S(2)}) copy-start(f32[4,1,32,32]{3,2,1,0:T(8,128)} %param.3) | copy-start | bytes 49156
  436.7 1.6 copy-start
Sparse Core Ops, SparseCore 0:
  12.9 213.4 all-gather.1
where the time goes:
time: 455 us
  blocking collectives  413 us (91%)
  local copies, waits for them, and re-layouts  18.2 us (4%)
  between operations  14.1 us (3%)
  matrix products  7.46 us (2%)
    squeeze x1, blocking collectives, local(): gathered_columns = gathered_columns[:, 0]  318 us
    all_gather x1, blocking collectives, local(): lax.all_gather(fill_columns, 'depth', axis=1, tiled=True)  46.5 us
    all_gather x1, blocking collectives, local(): lax.all_gather(columns, 'depth', axis=1, tiled=True)  18.9 us
    all_gather x1, blocking collectives, local(): squared_rows = lax.all_gather(squared, 'depth', axis=1, tiled=True)  15 us
    all_gather x1, blocking collectives, local(): lax.all_gather(density, 'depth', axis=1, tiled=True)  14.9 us
  transfers between devices with their start and end apart: 1, of which 0 were waited for; matrix products, arithmetic and copies ran while one was open for 1% of the time, Pallas kernels for 0%

commit v1 on v0

v1 whole, which is shorter than its diff:
```python
import jax
import jax.numpy as jnp
from jax import lax
from jax.experimental import pallas as pl
from jax.experimental.pallas import tpu as pltpu
from jax.sharding import Mesh, PartitionSpec as P

BS = 32
ROWS = 4
KF = 4
CB = 48
NCG = 8
LANES = 128
TILE = 40
AXES = ("zh", "x", "yh", "yl", "zl", "c")
SIZES = (3, 4, 4, 2, 4, 2)
NZ, NX, NYH, NYL, NL, NC = SIZES
NY = NYH * NYL
FIRST, SECOND = ("zh", "yh"), ("x", "yl")
NP, NS = NZ * NYH, NX * NYL
PIECE = NP * BS + 16
GROUP = NCG * KF * BS


def place(slab, codes, wanted):
    lane_slot = lax.broadcasted_iota(jnp.int32, (8, LANES), 1) // BS
    blocks, columns = [], []
    for code in codes:
        keep = lane_slot == (code & 3)
        block = slab[pl.ds(pl.multiple_of(code >> 14, 8), BS), :].reshape(BS // 8, 8, LANES)
        column = jnp.broadcast_to(slab[pl.ds((code >> 2) & 4095, 1), :], (8, LANES))
        blocks.append(jnp.where(keep, block, 0.0))
        columns.append(jnp.where(keep, column, 0.0)[None])
    every = jnp.concatenate(blocks + columns).reshape(-1, LANES)
    every = every + pltpu.roll(every, 64, 1)
    every = every + pltpu.roll(every, 32, 1)
    count = len(codes)
    blocks = every[: count * BS].reshape(count, BS // 8, 8, LANES)
    columns = every[count * BS :].reshape(count, 8, LANES)
    lands = columns == jnp.stack(wanted)
    return jnp.where(lands[:, None], blocks, 0.0).reshape(count * BS, LANES)


def wanted_of(tile, row):
    return jnp.broadcast_to(tile[BS + 1 + row : BS + 2 + row, :], (8, LANES))


def halves(values, axis):
    high = values.astype(jnp.bfloat16)
    low = (values - high.astype(jnp.float32)).astype(jnp.bfloat16)
    return jnp.concatenate([high, low], axis=axis)


def product(total):
    return (total[:BS, :LANES] + total[:BS, LANES:]) + (total[BS:, :LANES] + total[BS:, LANES:])


def pack_kernel(columns, fill, density, out, copies):
    lane_slot = lax.broadcasted_iota(jnp.int32, (8, LANES), 1) // BS
    line = lax.broadcasted_iota(jnp.int32, (8, LANES), 0)
    numbers = jnp.zeros((8, LANES), jnp.int32)
    for slot in range(ROWS):
        numbers = jnp.where((line == 0) & (lane_slot == slot), columns[0, slot], numbers)
    for row in range(ROWS):
        for slot in range(KF):
            numbers = jnp.where((line == row + 1) & (lane_slot == slot), fill[row, slot], numbers)
    numbers = numbers.astype(jnp.float32)
    data = jnp.concatenate([density[row] for row in range(ROWS)], axis=1)
    out[:BS, :] = data
    out[BS:, :] = numbers
    for n in range(NP):
        copies[n, :BS, :] = data
        copies[n, BS:, :] = numbers


def spread_kernel(plane, out):
    for member in range(NP):
        block = plane[member, :BS, :]
        column = plane[member, BS : BS + 1, :]
        for n in range(NS):
            out[n, member * BS : (member + 1) * BS, :] = block
            out[n, NP * BS + member : NP * BS + member + 1, :] = column
    for n in range(NS):
        out[n, NP * BS + NP :, :] = jnp.zeros((PIECE - NP * BS - NP, LANES), jnp.float32)


def square_kernel(codes, tile, left, slab, out, own, right):
    for row in range(0, ROWS, 2):
        wanted = [wanted_of(tile, row)] * NCG + [wanted_of(tile, row + 1)] * NCG
        blocks = place(slab, [codes[row * NCG + t] for t in range(2 * NCG)], wanted)
        right[row * NCG * BS : (row + 2) * NCG * BS, :] = halves(blocks, 1)
    for row in range(ROWS):
        values = right[row * NCG * BS : (row + 1) * NCG * BS, :]
        result = product(jnp.dot(halves(left[row], 0), values, preferred_element_type=jnp.float32))
        rows = slice(row * BS, (row + 1) * BS)
        own[rows, :] = result
        for n in range(NL):
            out[n, rows, :] = result


def right_kernel(codes, tile, slab, out):
    batch = 16
    for row in range(ROWS):
        wanted = [wanted_of(tile, row)] * batch
        for t in range(row * NCG * KF, (row + 1) * NCG * KF, batch):
            blocks = place(slab, [codes[t + n] for n in range(batch)], wanted)
            out[t * BS : (t + batch) * BS, :] = halves(blocks, 1)


def cube_kernel(mine, other, own, right, out):
    for row in range(ROWS):
        rows = slice(row * BS, (row + 1) * BS)
        total = jnp.zeros((2 * BS, 2 * LANES), jnp.float32)
        for near in range(NL):
            values = jnp.concatenate([mine[near, rows, :], other[near, rows, :]], axis=1)
            start = row * GROUP + near * NC * LANES
            total = total + jnp.dot(
                halves(values, 0), right[start : start + NC * LANES, :], preferred_element_type=jnp.float32
            )
        out[rows, :] = 3.0 * own[rows, :] - 2.0 * product(total)


def vmem():
    return pl.BlockSpec(memory_space=pltpu.VMEM)


def smem():
    return pl.BlockSpec(memory_space=pltpu.SMEM)


def call(kernel, name, shapes, specs, args, scratch=(), limit=16 * 2**20):
    size = 4 * sum(a.size for a in args)
    shapes = [jax.ShapeDtypeStruct(*shape) for shape in shapes]
    results = pl.pallas_call(
        kernel,
        out_shape=shapes,
        in_specs=specs,
        out_specs=[vmem() for _ in shapes],
        scratch_shapes=list(scratch),
        compiler_params=pltpu.CompilerParams(vmem_limit_bytes=limit),
        cost_estimate=pl.CostEstimate(flops=2**24, bytes_accessed=size, transcendentals=0),
        name=name,
    )(*args)
    return results if len(shapes) > 1 else results[0]


def codes_of(block_row):
    owner, slot = block_row // ROWS, block_row % ROWS
    piece = owner // NY % NX * NYL + owner % NYL
    member = owner // (NX * NY) * NYH + owner % NY // NYL
    return (piece * PIECE + member * BS) * 2**14 + (piece * PIECE + NP * BS + member) * 4 + slot


def local(density, columns, fill_columns):
    f32 = jnp.float32
    tile, copies = call(
        pack_kernel, "pack", [((TILE, LANES), f32), ((NP, TILE, LANES), f32)], [smem(), smem(), vmem()],
        (columns.reshape(1, ROWS), fill_columns.reshape(ROWS, KF), density.reshape(ROWS, BS, BS)),
        limit=60 * 2**20,
    )
    plane = lax.all_to_all(copies, FIRST, 0, 0)
    pair = lax.all_gather(tile, "c")
    plane, pair = lax.optimization_barrier((plane, pair))
    pieces = call(spread_kernel, "spread", [((NS, PIECE, LANES), f32)], [vmem()], (plane,))
    slab = lax.all_to_all(pieces, SECOND, 0, 0).reshape(NS * PIECE, LANES)

    near = [pair] + [
        lax.ppermute(pair, "zl", [(n, (n + step) % NL) for n in range(NL)]) for step in range(1, NL)
    ]
    rows = jnp.stack(near).reshape(NCG, TILE, LANES)
    numbers = rows[:, BS : BS + 5, ::BS].astype(jnp.int32)
    place_here, core = lax.axis_index("zl"), lax.axis_index("c")
    steps = jnp.arange(NCG, dtype=jnp.int32)
    groups = ((place_here - steps // NC) % NL * NC + steps % NC) * CB
    first = codes_of(numbers[:, 0, :].T + groups[None, :]).reshape(-1)
    second = codes_of(numbers[:, 1:, :].transpose(1, 0, 2) + groups[None, :, None])
    second = second.reshape(ROWS, NL, NC, KF)
    places = jnp.arange(NL, dtype=jnp.int32)
    turn = ((place_here - places[:, None]) % NL == places[None, :])[None, :, :, None, None]
    second = jnp.sum(jnp.where(turn, second[:, None], 0), axis=2)
    second = jnp.where(core == 0, second, second[:, :, ::-1]).reshape(-1)
    left = rows[:, :BS].reshape(NCG, BS, ROWS, BS).transpose(2, 1, 0, 3).reshape(ROWS, BS, NCG * BS)

    shape = (ROWS * BS, LANES)
    squared, own = call(
        square_kernel, "square", [((NL,) + shape, f32), (shape, f32)], [smem(), vmem(), vmem(), vmem()],
        (first, tile, left, slab),
        [pltpu.VMEM((ROWS * NCG * BS, 2 * LANES), jnp.bfloat16)],
    )
    right = call(
        right_kernel, "right", [((ROWS * GROUP, 2 * LANES), jnp.bfloat16)], [smem(), vmem(), vmem()],
        (second, tile, slab),
    )
    mine, right = lax.optimization_barrier((lax.all_to_all(squared, "zl", 0, 0), right))
    other = lax.ppermute(mine, "c", [(0, 1), (1, 0)])
    purified = call(cube_kernel, "cube", [(shape, f32)], [vmem()] * 4, (mine, other, own, right))
    return purified.reshape(ROWS, 1, BS, LANES)


def solution(mesh):
    fine = Mesh(mesh.devices.reshape(SIZES), AXES)
    grid, depth = ("zh", "x", "yh", "yl"), ("zl", "c")
    in_specs = (P(grid, depth, None, None), P(grid, depth, None), P(grid, depth, None))
    out_specs = P(grid, depth, None, None)
    return jax.shard_map(local, mesh=fine, in_specs=in_specs, out_specs=out_specs, check_vma=False)
```

time: 455 us -> 86.7 us (0.19)
  blocking collectives: 413 us -> 2.66 us
  starting transfers between devices: 0.01 us -> 53.4 us
  waiting for transfers between devices: 0.71 us -> 17.5 us
  local copies, waits for them, and re-layouts: 18.2 us -> 3.91 us
  between operations: 14.1 us -> 0.17 us
  Pallas kernels: 0 us -> 8.07 us
  matrix products: 7.46 us -> 0 us
    squeeze x1 -> x0, blocking collectives: 318 us -> none  [local(): gathered_columns = gathered_columns[:, 0]]
    all_gather x4 -> x1, blocking collectives: 95.3 us -> 2.66 us  [local(): pair = lax.all_gather(tile, 'c')]
    all_to_all x0 -> x3, starting transfers between devices: none -> 34.5 us  [the longest x1 19.8 us: local(): plane = lax.all_to_all(copies, FIRST, 0, 0)]
    ppermute x0 -> x4, starting transfers between devices: none -> 18.9 us  [the longest x3 13.3 us: local(): lax.ppermute(pair, 'zl', [(n, (n + step) % NL) for n in range(NL)])]
    all_to_all x0 -> x3, waiting for transfers between devices: none -> 11.7 us  [the longest x1 10.1 us: local(): plane = lax.all_to_all(copies, FIRST, 0, 0)]
    gather x4 -> x0, local copies, waits for them, and re-layouts: 10.1 us -> none  [the longest x1 4.8 us: local(): second_values = gathered[second_need]]
    pallas_call x0 -> x5, Pallas kernels: none -> 8.07 us  [call(): pl.pallas_call(kernel, out_shape=shapes, in_specs=specs, out_specs=[vmem(...]
    dot_general x4 -> x0, matrix products: 7.46 us -> none  [the longest x2 4.68 us: multiply_tile(): jnp.einsum('itab,itbsc->itsac', left_blocks, right, precision=lax.Precisi...]
  transfers between devices with their start and end apart: 1 -> 7, of which waited for: 0 -> 5; matrix products, arithmetic and copies ran while one was open for 1% -> 2% of each run, Pallas kernels for 0% -> 2%
where the time goes in v1:
time: 86.7 us; the launch traced here: 86.1 us
  starting transfers between devices  53.4 us (62%)
  waiting for transfers between devices  17.5 us (20%)
  Pallas kernels  8.07 us (9%)
  local copies, waits for them, and re-layouts  3.91 us (5%)
  blocking collectives  2.66 us (3%)
    all_to_all x1, starting transfers between devices, local(): plane = lax.all_to_all(copies, FIRST, 0, 0)  19.8 us
    ppermute x3, starting transfers between devices, local(): lax.ppermute(pair, 'zl', [(n, (n + step) % NL) for n in range(NL)])  13.3 us
    all_to_all x1, starting transfers between devices, local(): lax.all_to_all(squared, 'zl', 0, 0)  10.5 us
    all_to_all x1, waiting for transfers between devices, local(): plane = lax.all_to_all(copies, FIRST, 0, 0)  10.1 us
    pallas_call x5, Pallas kernels, call(): pl.pallas_call(kernel, out_shape=shapes, in_specs=specs, out_specs=[vmem(...  8.07 us
    ppermute x1, starting transfers between devices, local(): other = lax.ppermute(mine, 'c', [(0, 1), (1, 0)])  5.58 us
    ppermute x3, waiting for transfers between devices, local(): lax.ppermute(pair, 'zl', [(n, (n + step) % NL) for n in range(NL)])  4.62 us
    all_to_all x1, starting transfers between devices, local(): slab = lax.all_to_all(pieces, SECOND, 0, 0).reshape(NS * PIECE, LANES)  4.21 us
  transfers between devices with their start and end apart: 7, of which 5 were waited for; matrix products, arithmetic and copies ran while one was open for 2% of the time, Pallas kernels for 2%

profile of v1, /device:TPU:1, one launch (start us, length us, event | category | flops | bytes accessed | tf_op | source)
XLA Modules:
  0.0 86.1 jit_solution(3580394525478659312)
XLA Ops:
  0.0 1.7 %pack.1 = (f32[40,128]{1,0:T(8,128)}, f32[12,40,128]{2,1,0:T(8,128)}) custom-call(s32[1,4]{1,0:T(1,128)} %bitcast.68, s32[4,4]{1,0:T(4,128)} %bitcast.67, f32[4,32,32]{2,1,0:T(8,128)} %bitcast.62), custom_call_target="tpu_custom_call" | custom-call | flops 16777216 | bytes 16464 | tf_op jit(solution)/shard_map/pack/pallas_call | solution.py:134
  1.7 19.8 %all-to-all-start = ((f32[12,40,128]{2,1,0:T(8,128)}), f32[12,40,128]{2,1,0:T(8,128)S(1)}, u32[]{:S(2)}, u32[]{:S(2)}) async-start(f32[12,40,128]{2,1,0:T(8,128)} %get-tuple-element.13), calls=%async_computation | async-start | bytes 491520 | tf_op jit(solution)/shard_map/all_to_all | solution.py:161
  21.4 2.7 %all-gather = f32[80,128]{1,0:T(8,128)S(1)} all-gather(f32[40,128]{1,0:T(8,128)} %get-tuple-element.14.tile), channel_id=2, replica_groups=mesh['zh'=3,'x'=4,'yh'=4,'yl'=2,'zl'=4,'c'=2] {'c'}, dimensions={0}, use_global_device_ids=true | all-gather | bytes 61440 | tf_op jit(solution)/shard_map/all_gather | solution.py:162
  24.1 10.1 %all-to-all-done.plane = f32[12,40,128]{2,1,0:T(8,128)S(1)} async-done(((f32[12,40,128]{2,1,0:T(8,128)}), f32[12,40,128]{2,1,0:T(8,128)S(1)}, u32[]{:S(2)}, u32[]{:S(2)}) %all-to-all-start) | async-done | bytes 245792 | tf_op jit(solution)/shard_map/all_to_all | solution.py:161
  34.2 1.3 %spread.1 = f32[8,400,128]{2,1,0:T(8,128)} custom-call(f32[12,40,128]{2,1,0:T(8,128)S(1)} %all-to-all-done.plane), custom_call_target="tpu_custom_call" | custom-call | flops 16777216 | bytes 245760 | tf_op jit(solution)/shard_map/spread/pallas_call | solution.py:134
  35.5 4.2 %all-to-all-start.1 = ((f32[8,400,128]{2,1,0:T(8,128)}), f32[8,400,128]{2,1,0:T(8,128)S(1)}, u32[]{:S(2)}, u32[]{:S(2)}) async-start(f32[8,400,128]{2,1,0:T(8,128)} %spread.1), calls=%async_computation.1 | async-start | bytes 3276800 | tf_op jit(solution)/shard_map/all_to_all | solution.py:165
  39.8 9.2 %collective-permute-start.2 = (f32[2,40,128]{2,1,0:T(8,128)S(1)}, f32[2,40,128]{2,1,0:T(8,128)S(1)}, u32[]{:S(2)}, u32[]{:S(2)}) collective-permute-start(f32[2,40,128]{2,1,0:T(8,128)S(1)} %bitcast.55), channel_id=1, source_target_pairs={{0,6},{2,0},{4,2},{6,4},{1,7},{3,1},{5,3},{7,5},{8,14},{10,8},{12,... | collective-permute-start | bytes 122888 | tf_op jit(solution)/shard_map/ppermute | solution.py:168
  49.0 1.9 %collective-permute-start.1 = (f32[2,40,128]{2,1,0:T(8,128)S(1)}, f32[2,40,128]{2,1,0:T(8,128)S(1)}, u32[]{:S(2)}, u32[]{:S(2)}) collective-permute-start(f32[2,40,128]{2,1,0:T(8,128)S(1)} %bitcast.56), channel_id=1, source_target_pairs={{0,4},{2,6},{4,0},{6,2},{1,5},{3,7},{5,1},{7,3},{8,12},{10,14},{12... | collective-permute-start | bytes 122888 | tf_op jit(solution)/shard_map/ppermute | solution.py:168
  50.9 2.2 %collective-permute-start = (f32[2,40,128]{2,1,0:T(8,128)S(1)}, f32[2,40,128]{2,1,0:T(8,128)S(1)}, u32[]{:S(2)}, u32[]{:S(2)}) collective-permute-start(f32[2,40,128]{2,1,0:T(8,128)S(1)} %bitcast.57), channel_id=1, source_target_pairs={{0,2},{2,4},{4,6},{6,0},{1,3},{3,5},{5,7},{7,1},{8,10},{10,12},{12... | collective-permute-start | bytes 122888 | tf_op jit(solution)/shard_map/ppermute | solution.py:168
  53.2 0.0 collective-permute-done.2
  53.2 1.8 %collective-permute-done.1 = f32[2,40,128]{2,1,0:T(8,128)S(1)} collective-permute-done((f32[2,40,128]{2,1,0:T(8,128)S(1)}, f32[2,40,128]{2,1,0:T(8,128)S(1)}, u32[]{:S(2)}, u32[]{:S(2)}) %collective-permute-start.1) | collective-permute-done | bytes 40992 | tf_op jit(solution)/shard_map/ppermute | solution.py:168
  54.9 2.8 %collective-permute-done = f32[2,40,128]{2,1,0:T(8,128)S(1)} collective-permute-done((f32[2,40,128]{2,1,0:T(8,128)S(1)}, f32[2,40,128]{2,1,0:T(8,128)S(1)}, u32[]{:S(2)}, u32[]{:S(2)}) %collective-permute-start) | collective-permute-done | bytes 40992 | tf_op jit(solution)/shard_map/ppermute | solution.py:168
  57.8 0.0 copy-start.2
  57.8 0.1 copy.8
  57.9 0.1 slice.12
  58.0 0.1 copy.9
  58.1 0.1 reshape.149.codes
  58.2 0.3 reshape.150
  58.5 0.2 reshape.151.left
  58.7 0.0 all-to-all-done.1
  58.7 0.0 copy-done.2
  58.7 1.8 %square.1 = (f32[4,128,128]{2,1,0:T(8,128)}, f32[128,128]{1,0:T(8,128)S(1)}) custom-call(s32[32]{0:T(128)S(1)} %reshape.149.codes, f32[40,128]{1,0:T(8,128)S(1)} %copy-done.2, f32[4,32,256]{2,1,0:T(8,128)S(1)} %reshape.151.left, f32[3200,128]{1,0:T(8,128)S(1)} %bitcast.50), custom_call_target="tpu_custom_call" | custom-call | flops 16777216 | bytes 1790080 | tf_op jit(solution)/shard_map/square/pallas_call | solution.py:134
  60.6 10.5 %all-to-all-start.2 = ((f32[4,128,128]{2,1,0:T(8,128)}), f32[4,128,128]{2,1,0:T(8,128)S(1)}, u32[]{:S(2)}, u32[]{:S(2)}) async-start(f32[4,128,128]{2,1,0:T(8,128)} %get-tuple-element.17), calls=%async_computation.2 | async-start | bytes 524288 | tf_op jit(solution)/shard_map/all_to_all | solution.py:194
  71.1 0.1 iota_compare_fusion
  71.1 0.1 fusion.8
  71.3 0.1 select_reduce_fusion
  71.5 0.1 reshape.153.codes
  71.6 2.1 %right.1 = bf16[4096,256]{1,0:T(8,128)(2,1)S(1)} custom-call(s32[128]{0:T(128)S(1)} %reshape.153.codes, f32[40,128]{1,0:T(8,128)S(1)} %copy-done.2, f32[3200,128]{1,0:T(8,128)S(1)} %bitcast.51), custom_call_target="tpu_custom_call" | custom-call | flops 16777216 | bytes 1659392 | tf_op jit(solution)/shard_map/right/pallas_call | solution.py:134
  73.7 0.0 copy-start
  73.7 1.3 %copy-done = bf16[4096,256]{1,0:T(8,128)(2,1)} copy-done((bf16[4096,256]{1,0:T(8,128)(2,1)}, bf16[4096,256]{1,0:T(8,128)(2,1)S(1)}, u32[]{:S(2)}) %copy-start) | copy-done | bytes 2097176
  75.1 1.6 %all-to-all-done.2.mine = f32[4,128,128]{2,1,0:T(8,128)S(1)} async-done(((f32[4,128,128]{2,1,0:T(8,128)}), f32[4,128,128]{2,1,0:T(8,128)S(1)}, u32[]{:S(2)}, u32[]{:S(2)}) %all-to-all-start.2) | async-done | bytes 262176 | tf_op jit(solution)/shard_map/all_to_all | solution.py:194
  76.7 5.6 %collective-permute-start.3 = (f32[4,128,128]{2,1,0:T(8,128)S(1)}, f32[4,128,128]{2,1,0:T(8,128)S(1)}, u32[]{:S(2)}, u32[]{:S(2)}) collective-permute-start(f32[4,128,128]{2,1,0:T(8,128)S(1)} %all-to-all-done.2.mine), channel_id=1, source_target_pairs={{0,1},{1,0},{2,3},{3,2},{4,5},{5,4},{6,7},{7,6},{8,9},{9,8},{10,11... | collective-permute-start | bytes 786440 | tf_op jit(solution)/shard_map/ppermute | solution.py:195
  82.3 1.1 %collective-permute-done.3.other = f32[4,128,128]{2,1,0:T(8,128)S(1)} collective-permute-done((f32[4,128,128]{2,1,0:T(8,128)S(1)}, f32[4,128,128]{2,1,0:T(8,128)S(1)}, u32[]{:S(2)}, u32[]{:S(2)}) %collective-permute-start.3) | collective-permute-done | bytes 262176 | tf_op jit(solution)/shard_map/ppermute | solution.py:195
  83.4 0.0 copy-start.1
  83.4 1.6 %copy-done.1 = bf16[4096,256]{1,0:T(8,128)(2,1)S(1)} copy-done((bf16[4096,256]{1,0:T(8,128)(2,1)S(1)}, bf16[4096,256]{1,0:T(8,128)(2,1)}, u32[]{:S(2)}) %copy-start.1) | copy-done | bytes 2097176
  85.0 1.1 %cube.1 = f32[128,128]{1,0:T(8,128)} custom-call(f32[4,128,128]{2,1,0:T(8,128)S(1)} %all-to-all-done.2.mine, f32[4,128,128]{2,1,0:T(8,128)S(1)} %collective-permute-done.3.other, f32[128,128]{1,0:T(8,128)S(1)} %get-tuple-element.19.own, bf16[4096,256]{1,0:T(8,128)(2,1)S(1)} %copy-done.1), custom_call_target="tpu_custom_call" | custom-call | flops 16777216 | bytes 4784128 | tf_op jit(solution)/shard_map/cube/pallas_call | solution.py:134
  (11 shorter events, 0.2 us)
Async XLA Ops:
  1.7 32.6 %all-to-all-start = ((f32[12,40,128]{2,1,0:T(8,128)}), f32[12,40,128]{2,1,0:T(8,128)S(1)}, u32[]{:S(2)}, u32[]{:S(2)}) async-start(f32[12,40,128]{2,1,0:T(8,128)} %get-tuple-element.13), calls=%async_computation | async-start | bytes 491520 | tf_op jit(solution)/shard_map/all_to_all | solution.py:161
  35.5 23.2 %all-to-all-start.1 = ((f32[8,400,128]{2,1,0:T(8,128)}), f32[8,400,128]{2,1,0:T(8,128)S(1)}, u32[]{:S(2)}, u32[]{:S(2)}) async-start(f32[8,400,128]{2,1,0:T(8,128)} %spread.1), calls=%async_computation.1 | async-start | bytes 3276800 | tf_op jit(solution)/shard_map/all_to_all | solution.py:165
  39.8 13.4 %collective-permute-start.2 = (f32[2,40,128]{2,1,0:T(8,128)S(1)}, f32[2,40,128]{2,1,0:T(8,128)S(1)}, u32[]{:S(2)}, u32[]{:S(2)}) collective-permute-start(f32[2,40,128]{2,1,0:T(8,128)S(1)} %bitcast.55), channel_id=1, source_target_pairs={{0,6},{2,0},{4,2},{6,4},{1,7},{3,1},{5,3},{7,5},{8,14},{10,8},{12,... | collective-permute-start | bytes 122888 | tf_op jit(solution)/shard_map/ppermute | solution.py:168
  49.0 5.9 %collective-permute-start.1 = (f32[2,40,128]{2,1,0:T(8,128)S(1)}, f32[2,40,128]{2,1,0:T(8,128)S(1)}, u32[]{:S(2)}, u32[]{:S(2)}) collective-permute-start(f32[2,40,128]{2,1,0:T(8,128)S(1)} %bitcast.56), channel_id=1, source_target_pairs={{0,4},{2,6},{4,0},{6,2},{1,5},{3,7},{5,1},{7,3},{8,12},{10,14},{12... | collective-permute-start | bytes 122888 | tf_op jit(solution)/shard_map/ppermute | solution.py:168
  50.9 6.8 %collective-permute-start = (f32[2,40,128]{2,1,0:T(8,128)S(1)}, f32[2,40,128]{2,1,0:T(8,128)S(1)}, u32[]{:S(2)}, u32[]{:S(2)}) collective-permute-start(f32[2,40,128]{2,1,0:T(8,128)S(1)} %bitcast.57), channel_id=1, source_target_pairs={{0,2},{2,4},{4,6},{6,0},{1,3},{3,5},{5,7},{7,1},{8,10},{10,12},{12... | collective-permute-start | bytes 122888 | tf_op jit(solution)/shard_map/ppermute | solution.py:168
  57.8 1.0 %copy-start.2 = (f32[40,128]{1,0:T(8,128)S(1)}, f32[40,128]{1,0:T(8,128)}, u32[]{:S(2)}) copy-start(f32[40,128]{1,0:T(8,128)} %get-tuple-element.14.tile) | copy-start | bytes 61444
  60.6 16.1 %all-to-all-start.2 = ((f32[4,128,128]{2,1,0:T(8,128)}), f32[4,128,128]{2,1,0:T(8,128)S(1)}, u32[]{:S(2)}, u32[]{:S(2)}) async-start(f32[4,128,128]{2,1,0:T(8,128)} %get-tuple-element.17), calls=%async_computation.2 | async-start | bytes 524288 | tf_op jit(solution)/shard_map/all_to_all | solution.py:194
  73.7 1.3 %copy-start = (bf16[4096,256]{1,0:T(8,128)(2,1)}, bf16[4096,256]{1,0:T(8,128)(2,1)S(1)}, u32[]{:S(2)}) copy-start(bf16[4096,256]{1,0:T(8,128)(2,1)S(1)} %right.1) | copy-start | bytes 6291460
  76.7 6.7 %collective-permute-start.3 = (f32[4,128,128]{2,1,0:T(8,128)S(1)}, f32[4,128,128]{2,1,0:T(8,128)S(1)}, u32[]{:S(2)}, u32[]{:S(2)}) collective-permute-start(f32[4,128,128]{2,1,0:T(8,128)S(1)} %all-to-all-done.2.mine), channel_id=1, source_target_pairs={{0,1},{1,0},{2,3},{3,2},{4,5},{5,4},{6,7},{7,6},{8,9},{9,8},{10,11... | collective-permute-start | bytes 786440 | tf_op jit(solution)/shard_map/ppermute | solution.py:195
  83.4 1.6 %copy-start.1 = (bf16[4096,256]{1,0:T(8,128)(2,1)S(1)}, bf16[4096,256]{1,0:T(8,128)(2,1)}, u32[]{:S(2)}) copy-start(bf16[4096,256]{1,0:T(8,128)(2,1)} %copy-done) | copy-start | bytes 6291460
